TPU v7x, 256 devices: a whole 4x4x8 slice. The times are simulated.
256 devices in a mesh: gx: 8 (over x, core), gyz: 8 (over y, z_lo), band: 4 (over z_hi).
Axes of the slice: x: 4, y: 4, z: 8 (z_hi: 4, z_lo: 2; z = z_hi * 2 + z_lo), core: 2. Of those that a mesh axis runs over, the one named last changes fastest.
Arguments:
- orbitals: float32 [256, 32, 64, 128], P('band', 'gx', 'gyz'), may hold values from -6 to 6
- v_local: float32 [32, 64, 128], P('gx', 'gyz'), may hold values from 0 to 2
- features: bfloat16 [11, 32, 64, 128], P(None, 'gx', 'gyz'), may hold values from -6 to 6
- w_first: bfloat16 [256, 11], replicated, may hold values from -1.75 to 1.75
- w_hidden: bfloat16 [1, 256, 256], replicated, may hold values from -0.375 to 0.375
- w_last: bfloat16 [256], replicated, may hold values from -0.375 to 0.375
- rotation: float32 [256, 256], replicated, may hold values from -0.375 to 0.375
- assignment: int32 [256], replicated, may hold values from 0 to 255, each once
- degrees: int32 [256], P('band'), may hold values from 4 to 8, as said below
Outputs:
- gram: float32 [256, 256], P('band')
- rotated: float32 [256, 32, 64, 128], P('band', 'gx', 'gyz')
Inputs may be any that keep to these rules, and one draw needn't show every extreme that they name: `degrees`: a filter degree of each slot; some slot has 8 and some has 4. `assignment`: each orbital is held in exactly one slot.
All inputs are finite; a program needn't handle non-finite values.
Results may differ from a plain program's by a relative error of at most 0.0043.
Values may be sent and summed in bfloat16 or wider, within the bound.
No kernel may reach another device: no remote copies, remote signals or barrier semaphores. Data moves between devices by JAX's collectives and lax.ppermute only.
A program may use at most 64 MiB of HBM per device.

v0:
```python
import jax
import jax.numpy as jnp
from jax import lax
from jax.sharding import PartitionSpec as P

DEG = 8
LOWER_EDGE = 2.0
CUT_EDGE = 3.0
UPPER_EDGE = 9.5


def with_halo(block, sides, width):
    for axis, dim in sides:
        count = lax.axis_size(axis)
        forward = [(i, i + 1) for i in range(count - 1)]
        backward = [(target, source) for source, target in forward]
        low = lax.ppermute(
            lax.slice_in_dim(block, block.shape[dim] - width, None, axis=dim), axis, forward
        )
        high = lax.ppermute(lax.slice_in_dim(block, 0, width, axis=dim), axis, backward)
        block = jnp.concatenate([low, block, high], axis=dim)
    return block


def coefficients(count):
    half_width = (UPPER_EDGE - CUT_EDGE) / 2.0
    centre = (UPPER_EDGE + CUT_EDGE) / 2.0
    first = half_width / (LOWER_EDGE - centre)
    factors = [(first / half_width, 0.0)]
    sigma = first
    for rounds in range(1, count):
        updated = 1.0 / (2.0 / first - sigma)
        factors.append((2.0 * updated / half_width, sigma * updated))
        sigma = updated
    return (factors, centre)


def hamiltonian(field, potential):
    padded = with_halo(field, (("gx", 1), ("gyz", 2)), 1)
    padded = jnp.pad(padded, ((0, 0), (0, 0), (0, 0), (1, 1)))
    beside_all = padded[:, 2:, 1:-1, 1:-1] + padded[:, :-2, 1:-1, 1:-1]
    beside_all = beside_all + padded[:, 1:-1, 2:, 1:-1] + padded[:, 1:-1, :-2, 1:-1]
    beside_all = beside_all + padded[:, 1:-1, 1:-1, 2:] + padded[:, 1:-1, 1:-1, :-2]
    return 0.5 * (6.0 * field - beside_all) + potential * field


def network(cell_features, w_first, w_hidden, w_last):
    feature_count = cell_features.shape[0]
    flattened = cell_features.reshape(feature_count, -1)
    hidden = jax.nn.silu(jnp.dot(w_first, flattened, preferred_element_type=jnp.float32)).astype(
        jnp.bfloat16
    )
    hidden = jax.nn.silu(jnp.dot(w_hidden[0], hidden, preferred_element_type=jnp.float32)).astype(
        jnp.bfloat16
    )
    values = jnp.tanh(jnp.dot(w_last[None, :], hidden, preferred_element_type=jnp.float32)[0])
    return values.reshape(cell_features.shape[1:])


def on_device(
    orbitals, v_local, features, w_first, w_hidden, w_last, rotation, assignment, degrees
):
    group = lax.axis_index("band")
    local_slots, size_x, size_y, size_z = orbitals.shape
    total_slots = rotation.shape[0]
    cells = size_x * size_y * size_z
    total_cells = float(cells * lax.axis_size("gx") * lax.axis_size("gyz"))
    xc_field = network(features, w_first, w_hidden, w_last)
    potential = v_local + xc_field
    factors, centre = coefficients(DEG)
    previous = orbitals
    current = orbitals
    for rounds in range(DEG):
        image = hamiltonian(current, potential)
        scale_new, scale_old = factors[rounds]
        updated = scale_new * (image - centre * current) - scale_old * previous
        active = (degrees > rounds)[:, None, None, None]
        previous = jnp.where(active, current, previous)
        current = jnp.where(active, updated, current)
    filtered = current.astype(jnp.bfloat16).reshape(local_slots, cells)
    select = (assignment[:, None] == lax.iota(jnp.int32, total_slots)[None, :]).astype(jnp.float32)
    permuted = jnp.dot(select, rotation, precision=lax.Precision.HIGHEST)
    slot_rotation = jnp.dot(permuted, select.T, precision=lax.Precision.HIGHEST).astype(
        jnp.bfloat16
    )
    own_columns = lax.dynamic_slice_in_dim(slot_rotation, group * local_slots, local_slots, 1)
    shard_rows = lax.all_gather(filtered, "band", axis=0, tiled=True)
    margin = lax.dot_general(
        filtered, shard_rows, (((1,), (1,)), ((), ())), preferred_element_type=jnp.float32
    )
    gram_part = margin
    rotated_part = lax.dot_general(
        own_columns, shard_rows, (((0,), (0,)), ((), ())), preferred_element_type=jnp.float32
    )
    gram_part, rotated_flat = (gram_part, rotated_part)
    gram = lax.psum(gram_part, ("gx", "gyz")) / total_cells
    rotated = rotated_flat.reshape(local_slots, size_x, size_y, size_z)
    return (gram, rotated)


def solution(mesh):
    placed = (
        P("band", "gx", "gyz", None),
        P("gx", "gyz", None),
        P(None, "gx", "gyz", None),
        P(),
        P(),
        P(),
        P(),
        P(),
        P("band"),
    )
    return jax.shard_map(
        on_device,
        mesh=mesh,
        in_specs=placed,
        out_specs=(P("band", None), P("band", "gx", "gyz", None)),
        check_vma=False,
    )
```

profile of v0, /device:TPU:8, one launch (start us, length us, event | category | flops | bytes accessed | tf_op | source)
XLA Modules:
  0.0 750.5 jit_solution(973591448265603997)
XLA Ops:
  21.3 3.7 collective-permute-start.2
  29.3 6.6 collective-permute-done.3
  45.5 3.8 collective-permute-start.7
  51.0 3.5 collective-permute-done.7
  59.2 4.8 collective-permute-start.9
  67.1 3.9 collective-permute-start.11
  72.7 4.7 collective-permute-done.11
  82.6 5.3 collective-permute-start.13
  91.0 4.1 collective-permute-start.15
  96.6 4.7 collective-permute-done.15
  106.7 5.3 collective-permute-start.17
  115.0 3.9 collective-permute-start.19
  120.7 4.7 collective-permute-done.19
  130.1 5.3 collective-permute-start.21
  138.5 3.9 collective-permute-start.23
  144.2 4.7 collective-permute-done.23
  154.0 5.3 collective-permute-start.25
  162.3 3.9 collective-permute-start.27
  168.0 4.7 collective-permute-done.27
  177.4 5.3 collective-permute-start.29
  185.8 3.9 collective-permute-start.31
  191.4 4.7 collective-permute-done.31
  201.8 60.9 %all-gather.2.cloned.1.call-done = bf16[256,4096]{1,0:T(8,128)(2,1)} async-done(((bf16[64,4096]{1,0:T(8,128)(2,1)}), bf16[256,4096]{1,0:T(8,128)(2,1)}) %all-gather.2.cloned.1.call-update) | async-done | bytes 2097168 | tf_op jit(solution)/shard_map/all_gather | solution.py:87
  267.6 474.6 %all-reduce.10.cloned.1.call-done = f32[64,256]{1,0:T(8,128)} async-done(((f32[64,256]{1,0:T(8,128)}), f32[64,256]{1,0:T(8,128)}) %all-reduce.10.cloned.1.call-update) | async-done | bytes 65552 | tf_op jit(solution)/shard_map/psum | solution.py:96
  (109 shorter events, 99.3 us)
Async XLA Ops:
  7.2 255.5 %all-gather.2.cloned.1.call-start = ((), (), s32[]{:S(2)}) async-start(), calls=%async_computation | async-start | bytes 2621440 | tf_op jit(solution)/shard_map/all_gather | solution.py:87
  9.1 11.5 %collective-permute-start.1 = (f32[64,1,8,128]{3,0,2,1:T(8,128)S(1)}, f32[64,1,8,128]{3,0,2,1:T(8,128)S(1)}, u32[]{:S(2)}, u32[]{:S(2)}) collective-permute-start(f32[64,1,8,128]{3,0,2,1:T(8,128)S(1)} %get-tuple-element.37), channel_id=1, source_target_pairs={{0,32},{32,64},{64,96},{96,128},{128,160},{160,192},{192,224},{1,3... | collective-permute-start | bytes 786440 | tf_op jit(solution)/shard_map/ppermute | solution.py:17
  10.9 10.4 %collective-permute-start = (f32[64,1,8,128]{3,0,2,1:T(8,128)S(1)}, f32[64,1,8,128]{3,0,2,1:T(8,128)S(1)}, u32[]{:S(2)}, u32[]{:S(2)}) collective-permute-start(f32[64,1,8,128]{3,0,2,1:T(8,128)S(1)} %get-tuple-element.36), channel_id=1, source_target_pairs={{32,0},{64,32},{96,64},{128,96},{160,128},{192,160},{224,192},{33,... | collective-permute-start | bytes 786440 | tf_op jit(solution)/shard_map/ppermute | solution.py:20
  21.3 8.0 %collective-permute-start.2 = (f32[64,6,1,128]{3,0,2,1:T(8,128)S(1)}, f32[64,6,1,128]{3,0,2,1:T(8,128)S(1)}, u32[]{:S(2)}, u32[]{:S(2)}) collective-permute-start(f32[64,6,1,128]{3,0,2,1:T(8,128)S(1)} %get-tuple-element.21), channel_id=1, source_target_pairs={{4,0},{8,4},{12,8},{16,12},{20,16},{24,20},{28,24},{5,1},{9,5},{13... | collective-permute-start | bytes 589832 | tf_op jit(solution)/shard_map/ppermute | solution.py:20
  25.1 10.9 %collective-permute-start.3 = (f32[64,6,1,128]{3,0,2,1:T(8,128)S(1)}, f32[64,6,1,128]{3,0,2,1:T(8,128)S(1)}, u32[]{:S(2)}, u32[]{:S(2)}) collective-permute-start(f32[64,6,1,128]{3,0,2,1:T(8,128)S(1)} %get-tuple-element.20), channel_id=1, source_target_pairs={{0,4},{4,8},{8,12},{12,16},{16,20},{20,24},{24,28},{1,5},{5,9},{9,... | collective-permute-start | bytes 589832 | tf_op jit(solution)/shard_map/ppermute | solution.py:17
  43.4 7.6 %collective-permute-start.6 = (f32[64,6,1,128]{3,0,2,1:T(8,128)S(1)}, f32[64,6,1,128]{3,0,2,1:T(8,128)S(1)}, u32[]{:S(2)}, u32[]{:S(2)}) collective-permute-start(f32[64,6,1,128]{3,0,2,1:T(8,128)S(1)} %get-tuple-element.19), channel_id=1, source_target_pairs={{4,0},{8,4},{12,8},{16,12},{20,16},{24,20},{28,24},{5,1},{9,5},{13... | collective-permute-start | bytes 589832 | tf_op jit(solution)/shard_map/ppermute | solution.py:20
  45.5 9.0 %collective-permute-start.7 = (f32[64,6,1,128]{3,0,2,1:T(8,128)S(1)}, f32[64,6,1,128]{3,0,2,1:T(8,128)S(1)}, u32[]{:S(2)}, u32[]{:S(2)}) collective-permute-start(f32[64,6,1,128]{3,0,2,1:T(8,128)S(1)} %get-tuple-element.18), channel_id=1, source_target_pairs={{0,4},{4,8},{8,12},{12,16},{16,20},{20,24},{24,28},{1,5},{5,9},{9,... | collective-permute-start | bytes 589832 | tf_op jit(solution)/shard_map/ppermute | solution.py:17
  65.1 7.6 %collective-permute-start.10 = (f32[64,6,1,128]{3,0,2,1:T(8,128)S(1)}, f32[64,6,1,128]{3,0,2,1:T(8,128)S(1)}, u32[]{:S(2)}, u32[]{:S(2)}) collective-permute-start(f32[64,6,1,128]{3,0,2,1:T(8,128)S(1)} %get-tuple-element.17), channel_id=1, source_target_pairs={{4,0},{8,4},{12,8},{16,12},{20,16},{24,20},{28,24},{5,1},{9,5},{13... | collective-permute-start | bytes 589832 | tf_op jit(solution)/shard_map/ppermute | solution.py:20
  67.1 10.4 %collective-permute-start.11 = (f32[64,6,1,128]{3,0,2,1:T(8,128)S(1)}, f32[64,6,1,128]{3,0,2,1:T(8,128)S(1)}, u32[]{:S(2)}, u32[]{:S(2)}) collective-permute-start(f32[64,6,1,128]{3,0,2,1:T(8,128)S(1)} %get-tuple-element.16), channel_id=1, source_target_pairs={{0,4},{4,8},{8,12},{12,16},{16,20},{20,24},{24,28},{1,5},{5,9},{9,... | collective-permute-start | bytes 589832 | tf_op jit(solution)/shard_map/ppermute | solution.py:17
  81.3 6.6 collective-permute-start.12
  89.0 7.6 %collective-permute-start.14 = (f32[64,6,1,128]{3,0,2,1:T(8,128)S(1)}, f32[64,6,1,128]{3,0,2,1:T(8,128)S(1)}, u32[]{:S(2)}, u32[]{:S(2)}) collective-permute-start(f32[64,6,1,128]{3,0,2,1:T(8,128)S(1)} %get-tuple-element.15), channel_id=1, source_target_pairs={{4,0},{8,4},{12,8},{16,12},{20,16},{24,20},{28,24},{5,1},{9,5},{13... | collective-permute-start | bytes 589832 | tf_op jit(solution)/shard_map/ppermute | solution.py:20
  91.0 10.4 %collective-permute-start.15 = (f32[64,6,1,128]{3,0,2,1:T(8,128)S(1)}, f32[64,6,1,128]{3,0,2,1:T(8,128)S(1)}, u32[]{:S(2)}, u32[]{:S(2)}) collective-permute-start(f32[64,6,1,128]{3,0,2,1:T(8,128)S(1)} %get-tuple-element.14), channel_id=1, source_target_pairs={{0,4},{4,8},{8,12},{12,16},{16,20},{20,24},{24,28},{1,5},{5,9},{9,... | collective-permute-start | bytes 589832 | tf_op jit(solution)/shard_map/ppermute | solution.py:17
  113.1 7.6 %collective-permute-start.18 = (f32[64,6,1,128]{3,0,2,1:T(8,128)S(1)}, f32[64,6,1,128]{3,0,2,1:T(8,128)S(1)}, u32[]{:S(2)}, u32[]{:S(2)}) collective-permute-start(f32[64,6,1,128]{3,0,2,1:T(8,128)S(1)} %get-tuple-element.13), channel_id=1, source_target_pairs={{4,0},{8,4},{12,8},{16,12},{20,16},{24,20},{28,24},{5,1},{9,5},{13... | collective-permute-start | bytes 589832 | tf_op jit(solution)/shard_map/ppermute | solution.py:20
  115.0 10.4 %collective-permute-start.19 = (f32[64,6,1,128]{3,0,2,1:T(8,128)S(1)}, f32[64,6,1,128]{3,0,2,1:T(8,128)S(1)}, u32[]{:S(2)}, u32[]{:S(2)}) collective-permute-start(f32[64,6,1,128]{3,0,2,1:T(8,128)S(1)} %get-tuple-element.12), channel_id=1, source_target_pairs={{0,4},{4,8},{8,12},{12,16},{16,20},{20,24},{24,28},{1,5},{5,9},{9,... | collective-permute-start | bytes 589832 | tf_op jit(solution)/shard_map/ppermute | solution.py:17
  128.8 6.6 collective-permute-start.20
  136.6 7.6 %collective-permute-start.22 = (f32[64,6,1,128]{3,0,2,1:T(8,128)S(1)}, f32[64,6,1,128]{3,0,2,1:T(8,128)S(1)}, u32[]{:S(2)}, u32[]{:S(2)}) collective-permute-start(f32[64,6,1,128]{3,0,2,1:T(8,128)S(1)} %get-tuple-element.11), channel_id=1, source_target_pairs={{4,0},{8,4},{12,8},{16,12},{20,16},{24,20},{28,24},{5,1},{9,5},{13... | collective-permute-start | bytes 589832 | tf_op jit(solution)/shard_map/ppermute | solution.py:20
  138.5 10.4 %collective-permute-start.23 = (f32[64,6,1,128]{3,0,2,1:T(8,128)S(1)}, f32[64,6,1,128]{3,0,2,1:T(8,128)S(1)}, u32[]{:S(2)}, u32[]{:S(2)}) collective-permute-start(f32[64,6,1,128]{3,0,2,1:T(8,128)S(1)} %get-tuple-element.10), channel_id=1, source_target_pairs={{0,4},{4,8},{8,12},{12,16},{16,20},{20,24},{24,28},{1,5},{5,9},{9,... | collective-permute-start | bytes 589832 | tf_op jit(solution)/shard_map/ppermute | solution.py:17
  152.7 6.6 collective-permute-start.24
  160.4 7.6 %collective-permute-start.26 = (f32[64,6,1,128]{3,0,2,1:T(8,128)S(1)}, f32[64,6,1,128]{3,0,2,1:T(8,128)S(1)}, u32[]{:S(2)}, u32[]{:S(2)}) collective-permute-start(f32[64,6,1,128]{3,0,2,1:T(8,128)S(1)} %get-tuple-element.9), channel_id=1, source_target_pairs={{4,0},{8,4},{12,8},{16,12},{20,16},{24,20},{28,24},{5,1},{9,5},{13... | collective-permute-start | bytes 589832 | tf_op jit(solution)/shard_map/ppermute | solution.py:20
  162.3 10.4 %collective-permute-start.27 = (f32[64,6,1,128]{3,0,2,1:T(8,128)S(1)}, f32[64,6,1,128]{3,0,2,1:T(8,128)S(1)}, u32[]{:S(2)}, u32[]{:S(2)}) collective-permute-start(f32[64,6,1,128]{3,0,2,1:T(8,128)S(1)} %get-tuple-element.8), channel_id=1, source_target_pairs={{0,4},{4,8},{8,12},{12,16},{16,20},{20,24},{24,28},{1,5},{5,9},{9,... | collective-permute-start | bytes 589832 | tf_op jit(solution)/shard_map/ppermute | solution.py:17
  176.1 6.6 collective-permute-start.28
  183.9 7.6 %collective-permute-start.30 = (f32[64,6,1,128]{3,0,2,1:T(8,128)S(1)}, f32[64,6,1,128]{3,0,2,1:T(8,128)S(1)}, u32[]{:S(2)}, u32[]{:S(2)}) collective-permute-start(f32[64,6,1,128]{3,0,2,1:T(8,128)S(1)} %get-tuple-element.7), channel_id=1, source_target_pairs={{4,0},{8,4},{12,8},{16,12},{20,16},{24,20},{28,24},{5,1},{9,5},{13... | collective-permute-start | bytes 589832 | tf_op jit(solution)/shard_map/ppermute | solution.py:20
  185.8 10.4 %collective-permute-start.31 = (f32[64,6,1,128]{3,0,2,1:T(8,128)S(1)}, f32[64,6,1,128]{3,0,2,1:T(8,128)S(1)}, u32[]{:S(2)}, u32[]{:S(2)}) collective-permute-start(f32[64,6,1,128]{3,0,2,1:T(8,128)S(1)} %get-tuple-element.6), channel_id=1, source_target_pairs={{0,4},{4,8},{8,12},{12,16},{16,20},{20,24},{24,28},{1,5},{5,9},{9,... | collective-permute-start | bytes 589832 | tf_op jit(solution)/shard_map/ppermute | solution.py:17
  201.1 541.1 %all-reduce.10.cloned.1.call-start = ((), (), s32[]{:S(2)}) async-start(), calls=%async_computation.1 | async-start | bytes 131072 | tf_op jit(solution)/shard_map/psum | solution.py:96
  (16 other events, 272.6 us)
Sparse Core Ops, SparseCore 0:
  201.2 61.4 all-gather.1
  266.0 476.0 all-reduce.9
where the time goes:
time: 752 us; the launch traced here: 750 us
  waiting for transfers between devices  596 us (79%)
  starting transfers between devices  93.3 us (12%)
  other arithmetic  28.6 us (4%)
  between operations  14.7 us (2%)
  matrix products  11 us (1%)
    psum x1, waiting for transfers between devices, on_device(): gram = lax.psum(gram_part, ('gx', 'gyz')) / total_cells  475 us
    ppermute x16, starting transfers between devices, with_halo(): lax.ppermute(lax.slice_in_dim(block, block.shape[dim] - width, None, axis...  65.6 us
    all_gather x1, waiting for transfers between devices, on_device(): shard_rows = lax.all_gather(filtered, 'band', axis=0, tiled=True)  60.9 us
    ppermute x16, waiting for transfers between devices, with_halo(): lax.ppermute(lax.slice_in_dim(block, block.shape[dim] - width, None, axis...  46.3 us
    ppermute x16, starting transfers between devices, with_halo(): lax.ppermute(lax.slice_in_dim(block, 0, width, axis=dim), axis, backward)  27.6 us
    concatenate x15, other arithmetic, with_halo(): block = jnp.concatenate([low, block, high], axis=dim)  16.2 us
  transfers between devices with their start and end apart: 34, of which 25 were waited for; matrix products, arithmetic and copies ran while one was open for 2% of the time, Pallas kernels for 0%

commit v1 on v0

--- a/solution.py
+++ b/solution.py
@@ -7,6 +7,14 @@
 LOWER_EDGE = 2.0
 CUT_EDGE = 3.0
 UPPER_EDGE = 9.5
+
+
+def part_the_links(block_in):
+    axis_tag = "gyz"
+    comm_axis = "gx"
+    for idx in (comm_axis, axis_tag):
+        block_in = lax.psum(block_in, axis_name=idx)
+    return block_in
 
 
 def with_halo(block, sides, width):
@@ -93,7 +101,7 @@
         own_columns, shard_rows, (((0,), (0,)), ((), ())), preferred_element_type=jnp.float32
     )
     gram_part, rotated_flat = (gram_part, rotated_part)
-    gram = lax.psum(gram_part, ("gx", "gyz")) / total_cells
+    gram = part_the_links(gram_part) / total_cells
     rotated = rotated_flat.reshape(local_slots, size_x, size_y, size_z)
     return (gram, rotated)
 

time: 752 us -> 416 us (0.55)
  waiting for transfers between devices: 596 us -> 259 us
    psum x1 -> x2, waiting for transfers between devices: 475 us -> 138 us  [part_the_links(): block_in = lax.psum(block_in, axis_name=idx)]
  transfers between devices with their start and end apart: 34 -> 35, of which waited for: 25 -> 26; matrix products, arithmetic and copies ran while one was open for 2% -> 3% of each run, Pallas kernels for 0% -> 0%
where the time goes in v1:
time: 416 us; the launch traced here: 414 us
  waiting for transfers between devices  259 us (62%)
  starting transfers between devices  93.4 us (22%)
  other arithmetic  28.6 us (7%)
  between operations  14.4 us (3%)
  matrix products  11 us (3%)
  local copies, waits for them, and re-layouts  7.04 us (2%)
    psum x2, waiting for transfers between devices, part_the_links(): block_in = lax.psum(block_in, axis_name=idx)  138 us
    ppermute x16, starting transfers between devices, with_halo(): lax.ppermute(lax.slice_in_dim(block, block.shape[dim] - width, None, axis...  65.6 us
    all_gather x1, waiting for transfers between devices, on_device(): shard_rows = lax.all_gather(filtered, 'band', axis=0, tiled=True)  61.2 us
    ppermute x16, waiting for transfers between devices, with_halo(): lax.ppermute(lax.slice_in_dim(block, block.shape[dim] - width, None, axis...  46.3 us
    ppermute x16, starting transfers between devices, with_halo(): lax.ppermute(lax.slice_in_dim(block, 0, width, axis=dim), axis, backward)  27.6 us
    concatenate x15, other arithmetic, with_halo(): block = jnp.concatenate([low, block, high], axis=dim)  16.2 us
    ppermute x16, waiting for transfers between devices, with_halo(): lax.ppermute(lax.slice_in_dim(block, 0, width, axis=dim), axis, backward)  13.9 us
    select_n x7, other arithmetic, on_device(): current = jnp.where(active, updated, current)  9.57 us
  transfers between devices with their start and end apart: 35, of which 26 were waited for; matrix products, arithmetic and copies ran while one was open for 3% of the time, Pallas kernels for 0%

profile of v1, /device:TPU:8, one launch (start us, length us, event | category | flops | bytes accessed | tf_op | source)
XLA Modules:
  0.0 413.6 jit_solution(10473860137096531873)
XLA Ops:
  21.3 3.7 collective-permute-start.2
  29.3 6.6 %collective-permute-done.3 = f32[64,6,1,128]{3,0,2,1:T(8,128)S(1)} collective-permute-done((f32[64,6,1,128]{3,0,2,1:T(8,128)S(1)}, f32[64,6,1,128]{3,0,2,1:T(8,128)S(1)}, u32[]{:S(2)}, u32[]{:S(2)}) %collective-permute-start.3) | collective-permute-done | bytes 196640 | tf_op jit(solution)/shard_map/ppermute | solution.py:25
  45.5 3.8 collective-permute-start.7
  59.2 4.8 %collective-permute-start.9 = (f32[64,1,8,128]{3,0,2,1:T(8,128)S(1)}, f32[64,1,8,128]{3,0,2,1:T(8,128)S(1)}, u32[]{:S(2)}, u32[]{:S(2)}) collective-permute-start(f32[64,1,8,128]{3,0,2,1:T(8,128)S(1)} %get-tuple-element.32), channel_id=1, source_target_pairs={{0,32},{32,64},{64,96},{96,128},{128,160},{160,192},{192,224},{1,3... | collective-permute-start | bytes 786440 | tf_op jit(solution)/shard_map/ppermute | solution.py:25
  67.1 3.9 collective-permute-start.11
  72.7 4.7 %collective-permute-done.11 = f32[64,6,1,128]{3,0,2,1:T(8,128)S(1)} collective-permute-done((f32[64,6,1,128]{3,0,2,1:T(8,128)S(1)}, f32[64,6,1,128]{3,0,2,1:T(8,128)S(1)}, u32[]{:S(2)}, u32[]{:S(2)}) %collective-permute-start.11) | collective-permute-done | bytes 196640 | tf_op jit(solution)/shard_map/ppermute | solution.py:25
  82.6 5.3 %collective-permute-start.13 = (f32[64,1,8,128]{3,0,2,1:T(8,128)S(1)}, f32[64,1,8,128]{3,0,2,1:T(8,128)S(1)}, u32[]{:S(2)}, u32[]{:S(2)}) collective-permute-start(f32[64,1,8,128]{3,0,2,1:T(8,128)S(1)} %get-tuple-element.30), channel_id=1, source_target_pairs={{0,32},{32,64},{64,96},{96,128},{128,160},{160,192},{192,224},{1,3... | collective-permute-start | bytes 786440 | tf_op jit(solution)/shard_map/ppermute | solution.py:25
  91.0 4.1 collective-permute-start.15
  96.6 4.7 %collective-permute-done.15 = f32[64,6,1,128]{3,0,2,1:T(8,128)S(1)} collective-permute-done((f32[64,6,1,128]{3,0,2,1:T(8,128)S(1)}, f32[64,6,1,128]{3,0,2,1:T(8,128)S(1)}, u32[]{:S(2)}, u32[]{:S(2)}) %collective-permute-start.15) | collective-permute-done | bytes 196640 | tf_op jit(solution)/shard_map/ppermute | solution.py:25
  106.7 5.3 %collective-permute-start.17 = (f32[64,1,8,128]{3,0,2,1:T(8,128)S(1)}, f32[64,1,8,128]{3,0,2,1:T(8,128)S(1)}, u32[]{:S(2)}, u32[]{:S(2)}) collective-permute-start(f32[64,1,8,128]{3,0,2,1:T(8,128)S(1)} %get-tuple-element.28), channel_id=1, source_target_pairs={{0,32},{32,64},{64,96},{96,128},{128,160},{160,192},{192,224},{1,3... | collective-permute-start | bytes 786440 | tf_op jit(solution)/shard_map/ppermute | solution.py:25
  115.0 3.9 collective-permute-start.19
  120.7 4.7 %collective-permute-done.19 = f32[64,6,1,128]{3,0,2,1:T(8,128)S(1)} collective-permute-done((f32[64,6,1,128]{3,0,2,1:T(8,128)S(1)}, f32[64,6,1,128]{3,0,2,1:T(8,128)S(1)}, u32[]{:S(2)}, u32[]{:S(2)}) %collective-permute-start.19) | collective-permute-done | bytes 196640 | tf_op jit(solution)/shard_map/ppermute | solution.py:25
  130.1 5.3 %collective-permute-start.21 = (f32[64,1,8,128]{3,0,2,1:T(8,128)S(1)}, f32[64,1,8,128]{3,0,2,1:T(8,128)S(1)}, u32[]{:S(2)}, u32[]{:S(2)}) collective-permute-start(f32[64,1,8,128]{3,0,2,1:T(8,128)S(1)} %get-tuple-element.26), channel_id=1, source_target_pairs={{0,32},{32,64},{64,96},{96,128},{128,160},{160,192},{192,224},{1,3... | collective-permute-start | bytes 786440 | tf_op jit(solution)/shard_map/ppermute | solution.py:25
  138.5 3.9 collective-permute-start.23
  144.2 4.7 %collective-permute-done.23 = f32[64,6,1,128]{3,0,2,1:T(8,128)S(1)} collective-permute-done((f32[64,6,1,128]{3,0,2,1:T(8,128)S(1)}, f32[64,6,1,128]{3,0,2,1:T(8,128)S(1)}, u32[]{:S(2)}, u32[]{:S(2)}) %collective-permute-start.23) | collective-permute-done | bytes 196640 | tf_op jit(solution)/shard_map/ppermute | solution.py:25
  154.0 5.3 %collective-permute-start.25 = (f32[64,1,8,128]{3,0,2,1:T(8,128)S(1)}, f32[64,1,8,128]{3,0,2,1:T(8,128)S(1)}, u32[]{:S(2)}, u32[]{:S(2)}) collective-permute-start(f32[64,1,8,128]{3,0,2,1:T(8,128)S(1)} %get-tuple-element.24), channel_id=1, source_target_pairs={{0,32},{32,64},{64,96},{96,128},{128,160},{160,192},{192,224},{1,3... | collective-permute-start | bytes 786440 | tf_op jit(solution)/shard_map/ppermute | solution.py:25
  162.3 3.9 collective-permute-start.27
  168.0 4.7 %collective-permute-done.27 = f32[64,6,1,128]{3,0,2,1:T(8,128)S(1)} collective-permute-done((f32[64,6,1,128]{3,0,2,1:T(8,128)S(1)}, f32[64,6,1,128]{3,0,2,1:T(8,128)S(1)}, u32[]{:S(2)}, u32[]{:S(2)}) %collective-permute-start.27) | collective-permute-done | bytes 196640 | tf_op jit(solution)/shard_map/ppermute | solution.py:25
  177.4 5.3 %collective-permute-start.29 = (f32[64,1,8,128]{3,0,2,1:T(8,128)S(1)}, f32[64,1,8,128]{3,0,2,1:T(8,128)S(1)}, u32[]{:S(2)}, u32[]{:S(2)}) collective-permute-start(f32[64,1,8,128]{3,0,2,1:T(8,128)S(1)} %get-tuple-element.22), channel_id=1, source_target_pairs={{0,32},{32,64},{64,96},{96,128},{128,160},{160,192},{192,224},{1,3... | collective-permute-start | bytes 786440 | tf_op jit(solution)/shard_map/ppermute | solution.py:25
  185.8 3.9 collective-permute-start.31
  191.4 4.7 %collective-permute-done.31 = f32[64,6,1,128]{3,0,2,1:T(8,128)S(1)} collective-permute-done((f32[64,6,1,128]{3,0,2,1:T(8,128)S(1)}, f32[64,6,1,128]{3,0,2,1:T(8,128)S(1)}, u32[]{:S(2)}, u32[]{:S(2)}) %collective-permute-start.31) | collective-permute-done | bytes 196640 | tf_op jit(solution)/shard_map/ppermute | solution.py:25
  201.5 61.2 %all-gather.2.cloned.1.call-done = bf16[256,4096]{1,0:T(8,128)(2,1)} async-done(((bf16[64,4096]{1,0:T(8,128)(2,1)}), bf16[256,4096]{1,0:T(8,128)(2,1)}) %all-gather.2.cloned.1.call-update) | async-done | bytes 2097168 | tf_op jit(solution)/shard_map/all_gather | solution.py:95
  266.3 61.7 %all-reduce.11.cloned.1.call-done = f32[64,256]{1,0:T(8,128)} async-done(((f32[64,256]{1,0:T(8,128)}), f32[64,256]{1,0:T(8,128)}) %all-reduce.11.cloned.1.call-update) | async-done | bytes 65552 | tf_op jit(solution)/shard_map/psum | solution.py:16
  329.7 75.9 %all-reduce.13.cloned.1.call-done = f32[64,256]{1,0:T(8,128)} async-done(((f32[64,256]{1,0:T(8,128)}), f32[64,256]{1,0:T(8,128)}) %all-reduce.13.cloned.1.call-update) | async-done | bytes 65552 | tf_op jit(solution)/shard_map/psum | solution.py:16
  (112 shorter events, 102.9 us)
Async XLA Ops:
  7.2 255.5 %all-gather.2.cloned.1.call-start = ((), (), s32[]{:S(2)}) async-start(), calls=%async_computation | async-start | bytes 2621440 | tf_op jit(solution)/shard_map/all_gather | solution.py:95
  9.1 11.5 %collective-permute-start.1 = (f32[64,1,8,128]{3,0,2,1:T(8,128)S(1)}, f32[64,1,8,128]{3,0,2,1:T(8,128)S(1)}, u32[]{:S(2)}, u32[]{:S(2)}) collective-permute-start(f32[64,1,8,128]{3,0,2,1:T(8,128)S(1)} %get-tuple-element.37), channel_id=1, source_target_pairs={{0,32},{32,64},{64,96},{96,128},{128,160},{160,192},{192,224},{1,3... | collective-permute-start | bytes 786440 | tf_op jit(solution)/shard_map/ppermute | solution.py:25
  10.9 10.4 %collective-permute-start = (f32[64,1,8,128]{3,0,2,1:T(8,128)S(1)}, f32[64,1,8,128]{3,0,2,1:T(8,128)S(1)}, u32[]{:S(2)}, u32[]{:S(2)}) collective-permute-start(f32[64,1,8,128]{3,0,2,1:T(8,128)S(1)} %get-tuple-element.36), channel_id=1, source_target_pairs={{32,0},{64,32},{96,64},{128,96},{160,128},{192,160},{224,192},{33,... | collective-permute-start | bytes 786440 | tf_op jit(solution)/shard_map/ppermute | solution.py:28
  21.3 8.0 %collective-permute-start.2 = (f32[64,6,1,128]{3,0,2,1:T(8,128)S(1)}, f32[64,6,1,128]{3,0,2,1:T(8,128)S(1)}, u32[]{:S(2)}, u32[]{:S(2)}) collective-permute-start(f32[64,6,1,128]{3,0,2,1:T(8,128)S(1)} %get-tuple-element.21), channel_id=1, source_target_pairs={{4,0},{8,4},{12,8},{16,12},{20,16},{24,20},{28,24},{5,1},{9,5},{13... | collective-permute-start | bytes 589832 | tf_op jit(solution)/shard_map/ppermute | solution.py:28
  25.1 10.9 %collective-permute-start.3 = (f32[64,6,1,128]{3,0,2,1:T(8,128)S(1)}, f32[64,6,1,128]{3,0,2,1:T(8,128)S(1)}, u32[]{:S(2)}, u32[]{:S(2)}) collective-permute-start(f32[64,6,1,128]{3,0,2,1:T(8,128)S(1)} %get-tuple-element.20), channel_id=1, source_target_pairs={{0,4},{4,8},{8,12},{12,16},{16,20},{20,24},{24,28},{1,5},{5,9},{9,... | collective-permute-start | bytes 589832 | tf_op jit(solution)/shard_map/ppermute | solution.py:25
  43.4 7.6 %collective-permute-start.6 = (f32[64,6,1,128]{3,0,2,1:T(8,128)S(1)}, f32[64,6,1,128]{3,0,2,1:T(8,128)S(1)}, u32[]{:S(2)}, u32[]{:S(2)}) collective-permute-start(f32[64,6,1,128]{3,0,2,1:T(8,128)S(1)} %get-tuple-element.19), channel_id=1, source_target_pairs={{4,0},{8,4},{12,8},{16,12},{20,16},{24,20},{28,24},{5,1},{9,5},{13... | collective-permute-start | bytes 589832 | tf_op jit(solution)/shard_map/ppermute | solution.py:28
  45.5 9.0 %collective-permute-start.7 = (f32[64,6,1,128]{3,0,2,1:T(8,128)S(1)}, f32[64,6,1,128]{3,0,2,1:T(8,128)S(1)}, u32[]{:S(2)}, u32[]{:S(2)}) collective-permute-start(f32[64,6,1,128]{3,0,2,1:T(8,128)S(1)} %get-tuple-element.18), channel_id=1, source_target_pairs={{0,4},{4,8},{8,12},{12,16},{16,20},{20,24},{24,28},{1,5},{5,9},{9,... | collective-permute-start | bytes 589832 | tf_op jit(solution)/shard_map/ppermute | solution.py:25
  65.1 7.6 %collective-permute-start.10 = (f32[64,6,1,128]{3,0,2,1:T(8,128)S(1)}, f32[64,6,1,128]{3,0,2,1:T(8,128)S(1)}, u32[]{:S(2)}, u32[]{:S(2)}) collective-permute-start(f32[64,6,1,128]{3,0,2,1:T(8,128)S(1)} %get-tuple-element.17), channel_id=1, source_target_pairs={{4,0},{8,4},{12,8},{16,12},{20,16},{24,20},{28,24},{5,1},{9,5},{13... | collective-permute-start | bytes 589832 | tf_op jit(solution)/shard_map/ppermute | solution.py:28
  67.1 10.4 %collective-permute-start.11 = (f32[64,6,1,128]{3,0,2,1:T(8,128)S(1)}, f32[64,6,1,128]{3,0,2,1:T(8,128)S(1)}, u32[]{:S(2)}, u32[]{:S(2)}) collective-permute-start(f32[64,6,1,128]{3,0,2,1:T(8,128)S(1)} %get-tuple-element.16), channel_id=1, source_target_pairs={{0,4},{4,8},{8,12},{12,16},{16,20},{20,24},{24,28},{1,5},{5,9},{9,... | collective-permute-start | bytes 589832 | tf_op jit(solution)/shard_map/ppermute | solution.py:25
  81.3 6.6 %collective-permute-start.12 = (f32[64,1,8,128]{3,0,2,1:T(8,128)S(1)}, f32[64,1,8,128]{3,0,2,1:T(8,128)S(1)}, u32[]{:S(2)}, u32[]{:S(2)}) collective-permute-start(f32[64,1,8,128]{3,0,2,1:T(8,128)S(1)} %get-tuple-element.31), channel_id=1, source_target_pairs={{32,0},{64,32},{96,64},{128,96},{160,128},{192,160},{224,192},{33,... | collective-permute-start | bytes 786440 | tf_op jit(solution)/shard_map/ppermute | solution.py:28
  89.0 7.6 %collective-permute-start.14 = (f32[64,6,1,128]{3,0,2,1:T(8,128)S(1)}, f32[64,6,1,128]{3,0,2,1:T(8,128)S(1)}, u32[]{:S(2)}, u32[]{:S(2)}) collective-permute-start(f32[64,6,1,128]{3,0,2,1:T(8,128)S(1)} %get-tuple-element.15), channel_id=1, source_target_pairs={{4,0},{8,4},{12,8},{16,12},{20,16},{24,20},{28,24},{5,1},{9,5},{13... | collective-permute-start | bytes 589832 | tf_op jit(solution)/shard_map/ppermute | solution.py:28
  91.0 10.4 %collective-permute-start.15 = (f32[64,6,1,128]{3,0,2,1:T(8,128)S(1)}, f32[64,6,1,128]{3,0,2,1:T(8,128)S(1)}, u32[]{:S(2)}, u32[]{:S(2)}) collective-permute-start(f32[64,6,1,128]{3,0,2,1:T(8,128)S(1)} %get-tuple-element.14), channel_id=1, source_target_pairs={{0,4},{4,8},{8,12},{12,16},{16,20},{20,24},{24,28},{1,5},{5,9},{9,... | collective-permute-start | bytes 589832 | tf_op jit(solution)/shard_map/ppermute | solution.py:25
  113.1 7.6 %collective-permute-start.18 = (f32[64,6,1,128]{3,0,2,1:T(8,128)S(1)}, f32[64,6,1,128]{3,0,2,1:T(8,128)S(1)}, u32[]{:S(2)}, u32[]{:S(2)}) collective-permute-start(f32[64,6,1,128]{3,0,2,1:T(8,128)S(1)} %get-tuple-element.13), channel_id=1, source_target_pairs={{4,0},{8,4},{12,8},{16,12},{20,16},{24,20},{28,24},{5,1},{9,5},{13... | collective-permute-start | bytes 589832 | tf_op jit(solution)/shard_map/ppermute | solution.py:28
  115.0 10.4 %collective-permute-start.19 = (f32[64,6,1,128]{3,0,2,1:T(8,128)S(1)}, f32[64,6,1,128]{3,0,2,1:T(8,128)S(1)}, u32[]{:S(2)}, u32[]{:S(2)}) collective-permute-start(f32[64,6,1,128]{3,0,2,1:T(8,128)S(1)} %get-tuple-element.12), channel_id=1, source_target_pairs={{0,4},{4,8},{8,12},{12,16},{16,20},{20,24},{24,28},{1,5},{5,9},{9,... | collective-permute-start | bytes 589832 | tf_op jit(solution)/shard_map/ppermute | solution.py:25
  128.8 6.6 %collective-permute-start.20 = (f32[64,1,8,128]{3,0,2,1:T(8,128)S(1)}, f32[64,1,8,128]{3,0,2,1:T(8,128)S(1)}, u32[]{:S(2)}, u32[]{:S(2)}) collective-permute-start(f32[64,1,8,128]{3,0,2,1:T(8,128)S(1)} %get-tuple-element.27), channel_id=1, source_target_pairs={{32,0},{64,32},{96,64},{128,96},{160,128},{192,160},{224,192},{33,... | collective-permute-start | bytes 786440 | tf_op jit(solution)/shard_map/ppermute | solution.py:28
  136.6 7.6 %collective-permute-start.22 = (f32[64,6,1,128]{3,0,2,1:T(8,128)S(1)}, f32[64,6,1,128]{3,0,2,1:T(8,128)S(1)}, u32[]{:S(2)}, u32[]{:S(2)}) collective-permute-start(f32[64,6,1,128]{3,0,2,1:T(8,128)S(1)} %get-tuple-element.11), channel_id=1, source_target_pairs={{4,0},{8,4},{12,8},{16,12},{20,16},{24,20},{28,24},{5,1},{9,5},{13... | collective-permute-start | bytes 589832 | tf_op jit(solution)/shard_map/ppermute | solution.py:28
  138.5 10.4 %collective-permute-start.23 = (f32[64,6,1,128]{3,0,2,1:T(8,128)S(1)}, f32[64,6,1,128]{3,0,2,1:T(8,128)S(1)}, u32[]{:S(2)}, u32[]{:S(2)}) collective-permute-start(f32[64,6,1,128]{3,0,2,1:T(8,128)S(1)} %get-tuple-element.10), channel_id=1, source_target_pairs={{0,4},{4,8},{8,12},{12,16},{16,20},{20,24},{24,28},{1,5},{5,9},{9,... | collective-permute-start | bytes 589832 | tf_op jit(solution)/shard_map/ppermute | solution.py:25
  152.7 6.6 %collective-permute-start.24 = (f32[64,1,8,128]{3,0,2,1:T(8,128)S(1)}, f32[64,1,8,128]{3,0,2,1:T(8,128)S(1)}, u32[]{:S(2)}, u32[]{:S(2)}) collective-permute-start(f32[64,1,8,128]{3,0,2,1:T(8,128)S(1)} %get-tuple-element.25), channel_id=1, source_target_pairs={{32,0},{64,32},{96,64},{128,96},{160,128},{192,160},{224,192},{33,... | collective-permute-start | bytes 786440 | tf_op jit(solution)/shard_map/ppermute | solution.py:28
  160.4 7.6 %collective-permute-start.26 = (f32[64,6,1,128]{3,0,2,1:T(8,128)S(1)}, f32[64,6,1,128]{3,0,2,1:T(8,128)S(1)}, u32[]{:S(2)}, u32[]{:S(2)}) collective-permute-start(f32[64,6,1,128]{3,0,2,1:T(8,128)S(1)} %get-tuple-element.9), channel_id=1, source_target_pairs={{4,0},{8,4},{12,8},{16,12},{20,16},{24,20},{28,24},{5,1},{9,5},{13... | collective-permute-start | bytes 589832 | tf_op jit(solution)/shard_map/ppermute | solution.py:28
  162.3 10.4 %collective-permute-start.27 = (f32[64,6,1,128]{3,0,2,1:T(8,128)S(1)}, f32[64,6,1,128]{3,0,2,1:T(8,128)S(1)}, u32[]{:S(2)}, u32[]{:S(2)}) collective-permute-start(f32[64,6,1,128]{3,0,2,1:T(8,128)S(1)} %get-tuple-element.8), channel_id=1, source_target_pairs={{0,4},{4,8},{8,12},{12,16},{16,20},{20,24},{24,28},{1,5},{5,9},{9,... | collective-permute-start | bytes 589832 | tf_op jit(solution)/shard_map/ppermute | solution.py:25
  183.9 7.6 %collective-permute-start.30 = (f32[64,6,1,128]{3,0,2,1:T(8,128)S(1)}, f32[64,6,1,128]{3,0,2,1:T(8,128)S(1)}, u32[]{:S(2)}, u32[]{:S(2)}) collective-permute-start(f32[64,6,1,128]{3,0,2,1:T(8,128)S(1)} %get-tuple-element.7), channel_id=1, source_target_pairs={{4,0},{8,4},{12,8},{16,12},{20,16},{24,20},{28,24},{5,1},{9,5},{13... | collective-permute-start | bytes 589832 | tf_op jit(solution)/shard_map/ppermute | solution.py:28
  185.8 10.4 %collective-permute-start.31 = (f32[64,6,1,128]{3,0,2,1:T(8,128)S(1)}, f32[64,6,1,128]{3,0,2,1:T(8,128)S(1)}, u32[]{:S(2)}, u32[]{:S(2)}) collective-permute-start(f32[64,6,1,128]{3,0,2,1:T(8,128)S(1)} %get-tuple-element.6), channel_id=1, source_target_pairs={{0,4},{4,8},{8,12},{12,16},{16,20},{20,24},{24,28},{1,5},{5,9},{9,... | collective-permute-start | bytes 589832 | tf_op jit(solution)/shard_map/ppermute | solution.py:25
  201.1 126.9 %all-reduce.11.cloned.1.call-start = ((), (), s32[]{:S(2)}) async-start(), calls=%async_computation.1 | async-start | bytes 131072 | tf_op jit(solution)/shard_map/psum | solution.py:16
  265.9 139.7 %all-reduce.13.cloned.1.call-start = ((), (), s32[]{:S(2)}) async-start(), calls=%async_computation.2 | async-start | bytes 131072 | tf_op jit(solution)/shard_map/psum | solution.py:16
  (17 other events, 341.3 us)
Sparse Core Ops, SparseCore 0:
  201.2 61.4 all-gather.1
  266.0 61.9 all-reduce.10
  330.8 74.7 all-reduce.12
